TPU v7x, 32 devices: a whole 2x2x4 slice. The times are simulated.
32 devices in a mesh: groups: 2 (over x), tm: 16 (over z, y, core).
Axes of the slice: x: 2, y: 2, z: 4, core: 2. Of those that a mesh axis runs over, the one named last changes fastest.
Arguments:
- tokens: bfloat16 [2, 4096, 1152], P('groups', 'tm'), parts along dimension 0, may hold values from -6 to 6
- norm_gain: float32 [1152], replicated, may hold values from 0.5 to 8
- w_qkv: bfloat16 [1152, 1728], P('tm'), may hold values from -0.1875 to 0.1875
- w_out: bfloat16 [1152, 576], P('tm'), may hold values from -0.25 to 0.25
- block_mask: int32 [2, 2, 2], P('groups'), parts along dimension 0, may hold values from 0 to 1
- keep_tiles: int32 [2, 256], P('groups', 'tm'), parts along dimension 0, may hold values 0 or 1
- cotangent: bfloat16 [2, 4096, 1152], P('groups', 'tm'), parts along dimension 0, may hold values from -6 to 6
Outputs:
- mixed: bfloat16 [2, 4096, 1152], P('groups', 'tm'), parts along dimension 0
- grad_tokens: bfloat16 [2, 4096, 1152], P('groups', 'tm'), parts along dimension 0
- grad_qkv: float32 [2304, 1728], P(('groups', 'tm')), parts along dimension 0
- grad_out: float32 [2304, 576], P(('groups', 'tm')), parts along dimension 0
There are 2 independent parts, one for each index of `groups`. A program takes and returns all parts, laid end to end along the dimension named above; an argument that names none is the same for every part. Nothing has to cross between parts.
All inputs are finite; a program needn't handle non-finite values. No bound on the sum of `keep_tiles` on one device may be relied on, other than what follows from the above.
Results may differ from a plain program's by a relative error of at most 0.0055.
The roundings to bfloat16 on the way count: a program that leaves them out, or rounds other values in their place, can miss the bound.
Values may be sent and summed in bfloat16 or wider, within the bound.
A program may use at most 128 MiB of HBM per device.

v0:
```python
import jax
import jax.numpy as jnp
from jax import lax
from jax.sharding import PartitionSpec as P

HD = 72
SPLIT = 4
TB = 2
TILE = 16
EPS = 1e-06


def temporal(qkv_cols, dattn_cols, keep_cols, block_mask, frames):
    videos, per_owner, owners, _ = qkv_cols.shape
    band_count = owners // frames
    heads_n = dattn_cols.shape[-1] // HD
    scale = HD ** (-0.5)
    parts = qkv_cols.reshape(videos, per_owner, frames, band_count, 3, heads_n, HD)
    queries = parts[:, :, :, :, 0]
    key_part = parts[:, :, :, :, 1]
    val_part = parts[:, :, :, :, 2]
    d_out = dattn_cols.reshape(videos, per_owner, frames, band_count, heads_n, HD)
    frame_block = jnp.arange(frames) // TB
    blocks = jnp.repeat(jnp.repeat(block_mask, TB, 1), TB, 2) > 0
    same_block = frame_block[:, None] == frame_block[None, :]
    block_allow = blocks | same_block[None]
    kept = jnp.transpose(keep_cols.reshape(videos, per_owner, frames, band_count) > 0, (0, 1, 3, 2))
    diag_one = jnp.arange(frames)[:, None] == jnp.arange(frames)[None, :]
    allow = block_allow[:, None, None, None, :, :] & (kept[:, :, :, None, None, :] | diag_one)
    scores = (
        jnp.einsum("vrfshd,vrgshd->vrshfg", queries, key_part, preferred_element_type=jnp.float32)
        * scale
    )
    scores = jnp.where(allow, scores, -1e30)
    row_top = jnp.max(scores, -1, keepdims=True)
    expo = jnp.exp(scores - row_top)
    probs = expo / jnp.sum(expo, -1, keepdims=True)
    probs_b = probs.astype(jnp.bfloat16)
    attn = jnp.einsum(
        "vrshfg,vrgshd->vrfshd", probs_b, val_part, preferred_element_type=jnp.float32
    ).astype(jnp.bfloat16)
    dprob = jnp.einsum("vrfshd,vrgshd->vrshfg", d_out, val_part, preferred_element_type=jnp.float32)
    dscore = probs * (dprob - jnp.sum(probs * dprob, -1, keepdims=True))
    dscore_b = dscore.astype(jnp.bfloat16)
    grad_query = (
        jnp.einsum("vrshfg,vrgshd->vrfshd", dscore_b, key_part, preferred_element_type=jnp.float32)
        * scale
    ).astype(jnp.bfloat16)
    grad_key = (
        jnp.einsum("vrshfg,vrfshd->vrgshd", dscore_b, queries, preferred_element_type=jnp.float32)
        * scale
    ).astype(jnp.bfloat16)
    grad_value = jnp.einsum(
        "vrshfg,vrfshd->vrgshd", probs_b, d_out, preferred_element_type=jnp.float32
    ).astype(jnp.bfloat16)
    d_qkv = jnp.stack([grad_query, grad_key, grad_value], axis=4).reshape(
        videos, per_owner, owners, -1
    )
    return (attn.reshape(videos, per_owner, owners, -1), d_qkv)


def per_device(tokens, norm_gain, w_qkv, w_out, block_mask, keep_tiles, cotangent):
    owners = lax.axis_size("tm")
    videos, band_len, model_width = tokens.shape
    per_owner = band_len // owners
    frames = owners // SPLIT
    qkv_full, out_full = (
        lax.all_gather(w_qkv, "tm", axis=0, tiled=True),
        lax.all_gather(w_out, "tm", axis=0, tiled=True),
    )
    tok_float = tokens.astype(jnp.float32)
    inv_rms = lax.rsqrt(jnp.mean(tok_float * tok_float, -1, keepdims=True) + EPS)
    normed = tok_float * inv_rms
    hidden = (normed * norm_gain).astype(jnp.bfloat16)
    keep_tok = jnp.repeat(keep_tiles, TILE, axis=1).reshape(videos, per_owner, owners)
    qkv = jnp.dot(hidden, qkv_full, preferred_element_type=jnp.float32).astype(jnp.bfloat16)
    d_attn = jnp.dot(cotangent, out_full, preferred_element_type=jnp.float32).astype(jnp.bfloat16)
    qkv_cols, dattn_cols, keep_cols = (
        lax.all_to_all(
            qkv.reshape(videos, per_owner, owners, -1),
            "tm",
            split_axis=2,
            concat_axis=2,
            tiled=True,
        ),
        lax.all_to_all(
            d_attn.reshape(videos, per_owner, owners, -1),
            "tm",
            split_axis=2,
            concat_axis=2,
            tiled=True,
        ),
        lax.all_to_all(keep_tok, "tm", split_axis=2, concat_axis=2, tiled=True),
    )
    attn_cols, dqkv_cols = temporal(qkv_cols, dattn_cols, keep_cols, block_mask, frames)
    attn_rows, dqkv_rows = (
        lax.all_to_all(attn_cols, "tm", split_axis=2, concat_axis=2, tiled=True),
        lax.all_to_all(dqkv_cols, "tm", split_axis=2, concat_axis=2, tiled=True),
    )
    attn = attn_rows.reshape(videos, band_len, -1)
    d_qkv = dqkv_rows.reshape(videos, band_len, -1)
    part_qkv = jnp.einsum("vtd,vte->de", hidden, d_qkv, preferred_element_type=jnp.float32)
    part_out = jnp.einsum("vtd,vte->de", cotangent, attn, preferred_element_type=jnp.float32)
    d_hidden = lax.optimization_barrier(
        jnp.einsum("vte,de->vtd", d_qkv, qkv_full, preferred_element_type=jnp.float32).astype(
            jnp.bfloat16
        )
    )
    grad_qkv, grad_out = (
        lax.psum_scatter(part_qkv, "tm", scatter_dimension=0, tiled=True),
        lax.psum_scatter(part_out, "tm", scatter_dimension=0, tiled=True),
    )
    mixed = (
        tok_float + jnp.einsum("vte,de->vtd", attn, out_full, preferred_element_type=jnp.float32)
    ).astype(jnp.bfloat16)
    grad = d_hidden.astype(jnp.float32) * norm_gain
    grad_tokens = cotangent.astype(jnp.float32) + inv_rms * (
        grad - normed * jnp.mean(grad * normed, -1, keepdims=True)
    )
    return (mixed, grad_tokens.astype(jnp.bfloat16), grad_qkv, grad_out)


def solution(mesh):
    placed = (
        P("groups", "tm", None),
        P(),
        P("tm", None),
        P("tm", None),
        P("groups", None, None),
        P("groups", "tm"),
        P("groups", "tm", None),
    )
    return jax.shard_map(
        per_device,
        mesh=mesh,
        in_specs=placed,
        out_specs=(
            P("groups", "tm", None),
            P("groups", "tm", None),
            P(("groups", "tm"), None),
            P(("groups", "tm"), None),
        ),
        check_vma=False,
    )
```

profile of v0, /device:TPU:0, one launch (start us, length us, event | category | flops | bytes accessed | tf_op | source)
XLA Modules:
  0.0 400.1 jit_solution(6253478221850050072)
XLA Ops:
  7.2 0.7 all-gather.5.cloned.1.call-update
  7.9 0.7 all-gather.3.cloned.1.call-update
  8.6 1.3 broadcast_in_dim.16
  9.9 7.4 %all-to-all-start.1 = ((s32[1,16,16]{1,0,2:T(1,128)}), s32[1,16,16]{1,0,2:T(1,128)S(1)}, u32[]{:S(2)}, u32[]{:S(2)}) async-start(s32[1,16,16]{1,0,2:T(1,128)} %broadcast_in_dim.16), calls=%async_computation.1 | async-start | bytes 16384 | tf_op jit(solution)/shard_map/all_to_all | solution.py:93
  17.3 1.3 fusion.22
  18.6 33.7 %all-gather.5.cloned.1.call-done = bf16[1152,576]{1,0:T(8,128)(2,1)} async-done(((bf16[72,576]{1,0:T(8,128)(2,1)}), bf16[1152,576]{1,0:T(8,128)(2,1)}) %all-gather.5.cloned.1.call-update) | async-done | bytes 1327120 | tf_op jit(solution)/shard_map/all_gather | solution.py:69
  52.2 2.3 convolution_convert_fusion.4
  54.7 0.8 copy.64
  55.5 3.5 all-to-all-start.3
  59.1 48.6 %all-gather.3.cloned.1.call-done = bf16[1152,1728]{1,0:T(8,128)(2,1)} async-done(((bf16[72,1728]{1,0:T(8,128)(2,1)}), bf16[1152,1728]{1,0:T(8,128)(2,1)}) %all-gather.3.cloned.1.call-update) | async-done | bytes 3981328 | tf_op jit(solution)/shard_map/all_gather | solution.py:68
  107.7 4.0 convolution_convert_fusion.1
  111.7 0.6 copy.50
  112.3 1.3 copy.51
  113.6 3.9 all-to-all-start
  118.0 0.8 or_and_fusion
  118.7 1.3 reshape.295
  120.1 18.1 %all-to-all-done = bf16[1,16,16,1728]{3,1,0,2:T(8,128)(2,1)S(1)} async-done(((bf16[1,16,16,1728]{3,1,0,2:T(8,128)(2,1)}), bf16[1,16,16,1728]{3,1,0,2:T(8,128)(2,1)S(1)}, u32[]{:S(2)}, u32[]{:S(2)}) %all-to-all-start) | async-done | bytes 884768 | tf_op jit(solution)/shard_map/all_to_all | solution.py:79
  138.2 1.7 reshape.294
  139.9 1.4 fusion.34
  141.4 3.1 fusion.35
  144.5 0.9 fusion.14
  145.6 1.4 multiply_reduce_fusion
  147.0 0.6 multiply_convert_fusion
  147.7 0.4 copy-done.6
  148.1 0.8 fusion.12
  148.8 1.7 fusion.13
  150.6 1.1 reshape.289
  151.7 6.1 %all-to-all-start.2 = ((bf16[1,16,16,576]{3,1,0,2:T(8,128)(2,1)}), bf16[1,16,16,576]{3,1,0,2:T(8,128)(2,1)S(1)}, u32[]{:S(2)}, u32[]{:S(2)}) async-start(bf16[1,16,16,576]{3,1,0,2:T(8,128)(2,1)} %reshape.289), calls=%async_computation.2 | async-start | bytes 655360 | tf_op jit(solution)/shard_map/all_to_all | solution.py:97
  157.8 1.8 fusion.15
  159.6 1.5 pad_maximum_fusion
  161.1 0.3 copy.76
  161.4 1.9 reshape.290
  163.3 5.6 %all-to-all-done.2 = bf16[1,16,16,576]{3,1,0,2:T(8,128)(2,1)S(1)} async-done(((bf16[1,16,16,576]{3,1,0,2:T(8,128)(2,1)}), bf16[1,16,16,576]{3,1,0,2:T(8,128)(2,1)S(1)}, u32[]{:S(2)}, u32[]{:S(2)}) %all-to-all-start.2) | async-done | bytes 294944 | tf_op jit(solution)/shard_map/all_to_all | solution.py:97
  168.9 3.6 all-to-all-start.4
  172.7 2.0 convolution_bitcast_fusion
  174.8 23.5 %all-to-all-done.4 = bf16[1,16,16,1728]{3,1,0,2:T(8,128)(2,1)S(1)} async-done(((bf16[1,16,16,1728]{3,1,0,2:T(8,128)(2,1)}), bf16[1,16,16,1728]{3,1,0,2:T(8,128)(2,1)S(1)}, u32[]{:S(2)}, u32[]{:S(2)}) %all-to-all-start.4) | async-done | bytes 884768 | tf_op jit(solution)/shard_map/all_to_all | solution.py:98
  198.6 1.0 copy-done.3
  199.5 4.6 %fusion.31 = f32[1152,1728]{1,0:T(8,128)} fusion(bf16[256,1728]{1,0:T(8,128)(2,1)S(1)} %bitcast.103, bf16[1,256,1152]{2,1,0:T(8,128)(2,1)S(1)} %copy-done, f32[1152]{0:T(1024)S(1)} %copy-done.10, f32[256]{0:T(256)S(1)} %add_rsqrt_fusion), kind=kOutput, calls=%fused_computation.51 | convolution fusion | flops 1020395520 | bytes 9442816 | tf_op jit(solution)/shard_map/vtd,vte->de/dot_general | solution.py:102
  204.1 0.6 copy-done.12
  204.8 0.6 dynamic-slice
  206.0 1.5 fusion.2
  207.5 3.6 fusion.3
  211.1 0.3 fusion.17
  211.4 1.2 fusion.21
  212.7 73.5 %all-reduce.3.cloned.1.call-done = f32[1152,576]{0,1:T(8,128)} async-done(((f32[1152,576]{0,1:T(8,128)}), f32[1152,576]{0,1:T(8,128)}) %all-reduce.3.cloned.1.call-update) | async-done | bytes 2654224
  286.1 1.2 constant_dynamic-slice_fusion
  287.3 0.8 copy.72
  288.2 105.4 %reduce-scatter.3.cloned.1.call-done = f32[72,1728]{1,0:T(8,128)} async-done(((f32[1152,1728]{1,0:T(8,128)}), f32[72,1728]{1,0:T(8,128)}) %reduce-scatter.3.cloned.1.call-update) | async-done | bytes 497680 | tf_op jit(solution)/shard_map/reduce_scatter | solution.py:110
  (47 shorter events, 1.5 us)
Async XLA Ops:
  7.2 45.1 %all-gather.5.cloned.1.call-start = ((), (), s32[]{:S(2)}) async-start(), calls=%async_computation.7 | async-start | bytes 1566720 | tf_op jit(solution)/shard_map/all_gather | solution.py:69
  7.9 99.8 %all-gather.3.cloned.1.call-start = ((), (), s32[]{:S(2)}) async-start(), calls=%async_computation.6 | async-start | bytes 4386816 | tf_op jit(solution)/shard_map/all_gather | solution.py:68
  9.9 45.6 %all-to-all-start.1 = ((s32[1,16,16]{1,0,2:T(1,128)}), s32[1,16,16]{1,0,2:T(1,128)S(1)}, u32[]{:S(2)}, u32[]{:S(2)}) async-start(s32[1,16,16]{1,0,2:T(1,128)} %broadcast_in_dim.16), calls=%async_computation.1 | async-start | bytes 16384 | tf_op jit(solution)/shard_map/all_to_all | solution.py:93
  54.5 53.2 %copy-start = (bf16[1,256,1152]{2,1,0:T(8,128)(2,1)S(1)}, bf16[1,256,1152]{2,1,0:T(8,128)(2,1)}, u32[]{:S(2)}) copy-start(bf16[1,256,1152]{2,1,0:T(8,128)(2,1)} %param.7) | copy-start | bytes 1769476
  54.5 53.2 %copy-start.10 = (f32[1152]{0:T(1024)S(1)}, f32[1152]{0:T(1024)}, u32[]{:S(2)}) copy-start(f32[1152]{0:T(1024)} %param.8) | copy-start | bytes 13828
  55.5 58.1 %all-to-all-start.3 = ((bf16[1,16,16,576]{3,1,0,2:T(8,128)(2,1)}), bf16[1,16,16,576]{3,1,0,2:T(8,128)(2,1)S(1)}, u32[]{:S(2)}, u32[]{:S(2)}) async-start(bf16[1,16,16,576]{3,1,0,2:T(8,128)(2,1)} %copy.64), calls=%async_computation.3 | async-start | bytes 655360 | tf_op jit(solution)/shard_map/all_to_all | solution.py:86
  113.6 4.0 copy-start.11
  113.6 24.5 %all-to-all-start = ((bf16[1,16,16,1728]{3,1,0,2:T(8,128)(2,1)}), bf16[1,16,16,1728]{3,1,0,2:T(8,128)(2,1)S(1)}, u32[]{:S(2)}, u32[]{:S(2)}) async-start(bf16[1,16,16,1728]{3,1,0,2:T(8,128)(2,1)} %copy.51), calls=%async_computation | async-start | bytes 1835008 | tf_op jit(solution)/shard_map/all_to_all | solution.py:79
  141.4 3.1 copy-start.8
  144.4 2.6 copy-start.9
  144.4 1.1 copy-start.5
  147.0 1.0 copy-start.6
  151.7 17.2 %all-to-all-start.2 = ((bf16[1,16,16,576]{3,1,0,2:T(8,128)(2,1)}), bf16[1,16,16,576]{3,1,0,2:T(8,128)(2,1)S(1)}, u32[]{:S(2)}, u32[]{:S(2)}) async-start(bf16[1,16,16,576]{3,1,0,2:T(8,128)(2,1)} %reshape.289), calls=%async_computation.2 | async-start | bytes 655360 | tf_op jit(solution)/shard_map/all_to_all | solution.py:97
  157.8 1.8 copy-start.7
  163.3 9.4 %copy-start.2 = (bf16[1,256,1152]{2,1,0:T(8,128)(2,1)S(1)}, bf16[1,256,1152]{2,1,0:T(8,128)(2,1)}, u32[]{:S(2)}) copy-start(bf16[1,256,1152]{2,1,0:T(8,128)(2,1)} %param.13) | copy-start | bytes 1769476
  168.9 29.4 %all-to-all-start.4 = ((bf16[1,16,16,1728]{3,1,0,2:T(8,128)(2,1)}), bf16[1,16,16,1728]{3,1,0,2:T(8,128)(2,1)S(1)}, u32[]{:S(2)}, u32[]{:S(2)}) async-start(bf16[1,16,16,1728]{3,1,0,2:T(8,128)(2,1)} %reshape.290), calls=%async_computation.4 | async-start | bytes 1835008 | tf_op jit(solution)/shard_map/all_to_all | solution.py:98
  172.6 113.6 %all-reduce.3.cloned.1.call-start = ((), (), s32[]{:S(2)}) async-start(), calls=%async_computation.9 | async-start | bytes 5308416
  174.8 218.8 %reduce-scatter.3.cloned.1.call-start = ((), (), s32[]{:S(2)}) async-start(), calls=%async_computation.8 | async-start | bytes 8773632 | tf_op jit(solution)/shard_map/reduce_scatter | solution.py:110
  198.6 1.0 copy-start.3
  204.1 0.7 copy-start.12
  204.1 1.9 copy-start.1
  206.0 1.5 copy-start.4
Sparse Core Ops, SparseCore 0:
  10.1 42.0 all-gather.4
  54.5 53.1 all-gather.2
  177.0 109.1 all-reduce.2
  290.6 102.8 reduce-scatter.2
where the time goes:
time: 401 us; the launch traced here: 400 us
  waiting for transfers between devices  310 us (77%)
  matrix products  27.5 us (7%)
  starting transfers between devices  24.8 us (6%)
  local copies, waits for them, and re-layouts  17.5 us (4%)
  between operations  14.7 us (4%)
  other arithmetic  5.81 us (1%)
    reduce_scatter x1, waiting for transfers between devices, per_device(): lax.psum_scatter(part_qkv, 'tm', scatter_dimension=0, tiled=True)  105 us
    unnamed x5, waiting for transfers between devices  74.9 us
    all_gather x1, waiting for transfers between devices, per_device(): lax.all_gather(w_qkv, 'tm', axis=0, tiled=True)  48.6 us
    all_gather x1, waiting for transfers between devices, per_device(): lax.all_gather(w_out, 'tm', axis=0, tiled=True)  33.7 us
    all_to_all x1, waiting for transfers between devices, per_device(): lax.all_to_all(dqkv_cols, 'tm', split_axis=2, concat_axis=2, tiled=True)  23.5 us
    all_to_all x1, waiting for transfers between devices, per_device(): lax.all_to_all(qkv.reshape(videos, per_owner, owners, -1), 'tm', split_ax...  18.1 us
  transfers between devices with their start and end apart: 9, of which 7 were waited for; matrix products, arithmetic and copies ran while one was open for 9% of the time, Pallas kernels for 0%

commit v1 on v0

--- a/solution.py
+++ b/solution.py
@@ -8,6 +8,29 @@
 TB = 2
 TILE = 16
 EPS = 1e-06
+
+
+def in_blocks(x, dim, devices):
+    before, after = (x.shape[:dim], x.shape[dim + 1 :])
+    return jnp.moveaxis(x.reshape(*before, devices, -1, *after), dim, 0)
+
+
+def laid_out(parts, dim):
+    shape = list(parts.shape[1:])
+    shape[dim] *= parts.shape[0]
+    return jnp.moveaxis(parts, 0, dim).reshape(shape)
+
+
+def rotated_exchange(x, axis, split_dim, concat_dim):
+    length, index = (lax.axis_size(axis), lax.axis_index(axis))
+    tiles = in_blocks(x, split_dim, length)
+    result = tiles
+    for step in range(1, length):
+        target, source = ((index + step) % length, (index - step) % length)
+        sent = lax.dynamic_index_in_dim(tiles, target, 0)
+        partner_block = lax.ppermute(sent, axis, [(i, (i + step) % length) for i in range(length)])
+        result = lax.dynamic_update_slice_in_dim(result, partner_block, source, axis=0)
+    return laid_out(result, concat_dim)
 
 
 def temporal(qkv_cols, dattn_cols, keep_cols, block_mask, frames):
@@ -95,7 +118,7 @@
     attn_cols, dqkv_cols = temporal(qkv_cols, dattn_cols, keep_cols, block_mask, frames)
     attn_rows, dqkv_rows = (
         lax.all_to_all(attn_cols, "tm", split_axis=2, concat_axis=2, tiled=True),
-        lax.all_to_all(dqkv_cols, "tm", split_axis=2, concat_axis=2, tiled=True),
+        rotated_exchange(dqkv_cols, "tm", 2, 2),
     )
     attn = attn_rows.reshape(videos, band_len, -1)
     d_qkv = dqkv_rows.reshape(videos, band_len, -1)

time: 401 us -> 411 us (1.025)
  waiting for transfers between devices: 310 us -> 265 us
  local copies, waits for them, and re-layouts: 17.5 us -> 55.7 us
  starting transfers between devices: 24.8 us -> 40.5 us
    unnamed x5, waiting for transfers between devices: 74.9 us -> 17 us
    ppermute x0 -> x15, waiting for transfers between devices: none -> 35.8 us  [rotated_exchange(): lax.ppermute(sent, axis, [(i, (i + step) % length) for i in range(length)])]
    dynamic_update_slice x0 -> x15, local copies, waits for them, and re-layouts: none -> 35.1 us  [rotated_exchange(): lax.dynamic_update_slice_in_dim(result, partner_block, source, axis=0)]
    all_to_all x1 -> x0, waiting for transfers between devices: 23.5 us -> none  [per_device(): lax.all_to_all(dqkv_cols, 'tm', split_axis=2, concat_axis=2, tiled=True)]
    ppermute x0 -> x15, starting transfers between devices: none -> 19.3 us  [rotated_exchange(): lax.ppermute(sent, axis, [(i, (i + step) % length) for i in range(length)])]
  transfers between devices with their start and end apart: 9 -> 23, of which waited for: 7 -> 13; matrix products, arithmetic and copies ran while one was open for 9% -> 18% of each run, Pallas kernels for 0% -> 0%
where the time goes in v1:
time: 411 us; the launch traced here: 410 us
  waiting for transfers between devices  265 us (64%)
  local copies, waits for them, and re-layouts  55.7 us (14%)
  starting transfers between devices  40.5 us (10%)
  matrix products  26.7 us (6%)
  between operations  15.2 us (4%)
  other arithmetic  6.83 us (2%)
    reduce_scatter x1, waiting for transfers between devices, per_device(): lax.psum_scatter(part_qkv, 'tm', scatter_dimension=0, tiled=True)  105 us
    all_gather x1, waiting for transfers between devices, per_device(): lax.all_gather(w_qkv, 'tm', axis=0, tiled=True)  48.6 us
    ppermute x15, waiting for transfers between devices, rotated_exchange(): lax.ppermute(sent, axis, [(i, (i + step) % length) for i in range(length)])  35.8 us
    dynamic_update_slice x15, local copies, waits for them, and re-layouts, rotated_exchange(): lax.dynamic_update_slice_in_dim(result, partner_block, source, axis=0)  35.1 us
    all_gather x1, waiting for transfers between devices, per_device(): lax.all_gather(w_out, 'tm', axis=0, tiled=True)  33.7 us
    ppermute x15, starting transfers between devices, rotated_exchange(): lax.ppermute(sent, axis, [(i, (i + step) % length) for i in range(length)])  19.3 us
    all_to_all x1, waiting for transfers between devices, per_device(): lax.all_to_all(qkv.reshape(videos, per_owner, owners, -1), 'tm', split_ax...  18 us
    unnamed x5, waiting for transfers between devices  17 us
  transfers between devices with their start and end apart: 23, of which 13 were waited for; matrix products, arithmetic and copies ran while one was open for 18% of the time, Pallas kernels for 0%

profile of v1, /device:TPU:0, one launch (start us, length us, event | category | flops | bytes accessed | tf_op | source)
XLA Modules:
  0.0 409.6 jit_solution(15881253793933997631)
XLA Ops:
  9.9 7.4 %all-to-all-start.1 = ((s32[1,16,16]{1,0,2:T(1,128)}), s32[1,16,16]{1,0,2:T(1,128)S(1)}, u32[]{:S(2)}, u32[]{:S(2)}) async-start(s32[1,16,16]{1,0,2:T(1,128)} %broadcast_in_dim.16), calls=%async_computation.1 | async-start | bytes 16384 | tf_op jit(solution)/shard_map/all_to_all | solution.py:116
  18.6 33.7 %all-gather.5.cloned.1.call-done = bf16[1152,576]{1,0:T(8,128)(2,1)} async-done(((bf16[72,576]{1,0:T(8,128)(2,1)}), bf16[1152,576]{1,0:T(8,128)(2,1)}) %all-gather.5.cloned.1.call-update) | async-done | bytes 1327120 | tf_op jit(solution)/shard_map/all_gather | solution.py:92
  52.2 2.3 convolution_convert_fusion.4
  55.5 3.5 all-to-all-start.3
  59.1 48.6 %all-gather.3.cloned.1.call-done = bf16[1152,1728]{1,0:T(8,128)(2,1)} async-done(((bf16[72,1728]{1,0:T(8,128)(2,1)}), bf16[1152,1728]{1,0:T(8,128)(2,1)}) %all-gather.3.cloned.1.call-update) | async-done | bytes 3981328 | tf_op jit(solution)/shard_map/all_gather | solution.py:91
  107.7 4.0 convolution_convert_fusion.1
  113.6 3.8 all-to-all-start
  120.2 18.0 %all-to-all-done = bf16[1,16,16,1728]{3,1,0,2:T(8,128)(2,1)S(1)} async-done(((bf16[1,16,16,1728]{3,1,0,2:T(8,128)(2,1)}), bf16[1,16,16,1728]{3,1,0,2:T(8,128)(2,1)S(1)}, u32[]{:S(2)}, u32[]{:S(2)}) %all-to-all-start) | async-done | bytes 884768 | tf_op jit(solution)/shard_map/all_to_all | solution.py:102
  138.2 1.7 reshape.303
  139.9 1.4 fusion.34
  141.4 3.2 fusion.35
  146.7 6.1 %all-to-all-start.2 = ((bf16[1,16,16,576]{3,1,0,2:T(8,128)(2,1)}), bf16[1,16,16,576]{3,1,0,2:T(8,128)(2,1)S(1)}, u32[]{:S(2)}, u32[]{:S(2)}) async-start(bf16[1,16,16,576]{3,1,0,2:T(8,128)(2,1)} %reshape.299), calls=%async_computation.2 | async-start | bytes 655360 | tf_op jit(solution)/shard_map/all_to_all | solution.py:120
  154.5 1.6 fusion.15
  156.0 1.7 multiply_convert_fusion
  157.7 6.2 %all-to-all-done.2 = bf16[1,16,16,576]{3,1,0,2:T(8,128)(2,1)S(1)} async-done(((bf16[1,16,16,576]{3,1,0,2:T(8,128)(2,1)}), bf16[1,16,16,576]{3,1,0,2:T(8,128)(2,1)S(1)}, u32[]{:S(2)}, u32[]{:S(2)}) %all-to-all-start.2) | async-done | bytes 294944 | tf_op jit(solution)/shard_map/all_to_all | solution.py:120
  164.0 2.1 convolution_bitcast_fusion
  168.9 1.5 pad_maximum_fusion
  171.9 2.9 dynamic-slice_bitcast_fusion
  175.2 2.1 collective-permute-start.8
  177.9 1.6 collective-permute-start.6
  179.5 3.0 collective-permute-start.5
  183.8 2.0 collective-permute-start.4
  187.0 8.9 %collective-permute-start.3 = (bf16[1,1,16,1,1728]{4,0,2,3,1:T(2,128)(2,1)S(1)}, bf16[1,1,16,1,1728]{4,0,2,3,1:T(2,128)(2,1)S(1)}, u32[]{:S(2)}, u32[]{:S(2)}) collective-permute-start(bf16[1,1,16,1,1728]{4,0,2,3,1:T(2,128)(2,1)S(1)} %get-tuple-element.34), channel_id=1, source_target_pairs={{0,4},{1,5},{2,6},{3,7},{4,8},{5,9},{6,10},{7,11},{8,12},{9,13},{1... | collective-permute-start | bytes 165896 | tf_op jit(solution)/shard_map/ppermute | solution.py:31
  195.9 14.3 %collective-permute-done.7 = bf16[1,1,16,1,1728]{4,0,2,3,1:T(2,128)(2,1)S(1)} collective-permute-done((bf16[1,1,16,1,1728]{4,0,2,3,1:T(2,128)(2,1)S(1)}, bf16[1,1,16,1,1728]{4,0,2,3,1:T(2,128)(2,1)S(1)}, u32[]{:S(2)}, u32[]{:S(2)}) %collective-permute-start.7) | collective-permute-done | bytes 55328 | tf_op jit(solution)/shard_map/ppermute | solution.py:31
  210.3 3.6 collective-permute-done.6
  213.9 7.9 %collective-permute-done.5 = bf16[1,1,16,1,1728]{4,0,2,3,1:T(2,128)(2,1)S(1)} collective-permute-done((bf16[1,1,16,1,1728]{4,0,2,3,1:T(2,128)(2,1)S(1)}, bf16[1,1,16,1,1728]{4,0,2,3,1:T(2,128)(2,1)S(1)}, u32[]{:S(2)}, u32[]{:S(2)}) %collective-permute-start.5) | collective-permute-done | bytes 55328 | tf_op jit(solution)/shard_map/ppermute | solution.py:31
  221.8 3.2 collective-permute-done.4
  225.9 4.0 collective-permute-done
  230.6 2.9 dynamic_update_slice.45
  233.6 2.3 dynamic_update_slice.46
  235.9 2.3 dynamic_update_slice.47
  238.2 2.3 dynamic_update_slice.48
  240.5 2.3 dynamic_update_slice.49
  242.8 2.3 dynamic_update_slice.50
  245.1 2.3 dynamic_update_slice.51
  247.4 2.3 dynamic_update_slice.52
  249.7 2.3 dynamic_update_slice.53
  252.0 2.3 dynamic_update_slice.54
  254.3 2.3 dynamic_update_slice.55
  256.6 2.3 dynamic_update_slice.56
  259.0 2.3 dynamic_update_slice.57
  261.3 2.3 dynamic_update_slice.58
  263.6 2.3 dynamic_update_slice.59
  265.9 4.6 %fusion.31 = f32[1152,1728]{1,0:T(8,128)} fusion(bf16[256,1728]{1,0:T(8,128)(2,1)S(1)} %bitcast.135, bf16[1,256,1152]{2,1,0:T(8,128)(2,1)S(1)} %copy-done, f32[1152]{0:T(1024)S(1)} %copy-done.11, f32[256]{0:T(256)S(1)} %add_rsqrt_fusion), kind=kOutput, calls=%fused_computation.51 | convolution fusion | flops 1020395520 | bytes 9442816 | tf_op jit(solution)/shard_map/vtd,vte->de/dot_general | solution.py:125
  272.4 3.6 fusion.3
  278.6 1.5 fusion.2
  280.1 15.6 %all-reduce.3.cloned.1.call-done = f32[1152,576]{0,1:T(8,128)} async-done(((f32[1152,576]{0,1:T(8,128)}), f32[1152,576]{0,1:T(8,128)}) %all-reduce.3.cloned.1.call-update) | async-done | bytes 2654224
  297.7 105.4 %reduce-scatter.3.cloned.1.call-done = f32[72,1728]{1,0:T(8,128)} async-done(((f32[1152,1728]{1,0:T(8,128)}), f32[72,1728]{1,0:T(8,128)}) %reduce-scatter.3.cloned.1.call-update) | async-done | bytes 497680 | tf_op jit(solution)/shard_map/reduce_scatter | solution.py:133
  (96 shorter events, 28.3 us)
Async XLA Ops:
  7.2 45.1 %all-gather.5.cloned.1.call-start = ((), (), s32[]{:S(2)}) async-start(), calls=%async_computation.6 | async-start | bytes 1566720 | tf_op jit(solution)/shard_map/all_gather | solution.py:92
  7.9 99.8 %all-gather.3.cloned.1.call-start = ((), (), s32[]{:S(2)}) async-start(), calls=%async_computation.5 | async-start | bytes 4386816 | tf_op jit(solution)/shard_map/all_gather | solution.py:91
  9.9 45.6 %all-to-all-start.1 = ((s32[1,16,16]{1,0,2:T(1,128)}), s32[1,16,16]{1,0,2:T(1,128)S(1)}, u32[]{:S(2)}, u32[]{:S(2)}) async-start(s32[1,16,16]{1,0,2:T(1,128)} %broadcast_in_dim.16), calls=%async_computation.1 | async-start | bytes 16384 | tf_op jit(solution)/shard_map/all_to_all | solution.py:116
  54.5 53.2 %copy-start = (bf16[1,256,1152]{2,1,0:T(8,128)(2,1)S(1)}, bf16[1,256,1152]{2,1,0:T(8,128)(2,1)}, u32[]{:S(2)}) copy-start(bf16[1,256,1152]{2,1,0:T(8,128)(2,1)} %param.7) | copy-start | bytes 1769476
  54.5 53.2 %copy-start.11 = (f32[1152]{0:T(1024)S(1)}, f32[1152]{0:T(1024)}, u32[]{:S(2)}) copy-start(f32[1152]{0:T(1024)} %param.8) | copy-start | bytes 13828
  55.5 58.1 %all-to-all-start.3 = ((bf16[1,16,16,576]{3,1,0,2:T(8,128)(2,1)}), bf16[1,16,16,576]{3,1,0,2:T(8,128)(2,1)S(1)}, u32[]{:S(2)}, u32[]{:S(2)}) async-start(bf16[1,16,16,576]{3,1,0,2:T(8,128)(2,1)} %copy.63), calls=%async_computation.3 | async-start | bytes 655360 | tf_op jit(solution)/shard_map/all_to_all | solution.py:109
  113.6 4.0 copy-start.14
  113.6 24.5 %all-to-all-start = ((bf16[1,16,16,1728]{3,1,0,2:T(8,128)(2,1)}), bf16[1,16,16,1728]{3,1,0,2:T(8,128)(2,1)S(1)}, u32[]{:S(2)}, u32[]{:S(2)}) async-start(bf16[1,16,16,1728]{3,1,0,2:T(8,128)(2,1)} %copy.50), calls=%async_computation | async-start | bytes 1835008 | tf_op jit(solution)/shard_map/all_to_all | solution.py:102
  139.9 1.5 copy-start.13
  141.4 3.2 copy-start.5
  141.4 3.2 copy-start.9
  144.6 9.9 %copy-start.10 = (f32[16,4,8,4]{3,2,1,0:T(8,128)}, f32[16,4,8,4]{3,2,1,0:T(8,128)S(1)}, u32[]{:S(2)}) copy-start(f32[16,4,8,4]{3,2,1,0:T(8,128)S(1)} %get-tuple-element.38) | copy-start | bytes 24580
  145.5 7.6 %copy-start.4 = (bf16[16,4,4,8,72]{4,3,0,2,1:T(8,128)(2,1)S(1)}, bf16[16,4,4,8,72]{4,3,0,2,1:T(8,128)(2,1)}, u32[]{:S(2)}) copy-start(bf16[16,4,4,8,72]{4,3,0,2,1:T(8,128)(2,1)} %reshape.304) | copy-start | bytes 884740
  146.7 17.2 %all-to-all-start.2 = ((bf16[1,16,16,576]{3,1,0,2:T(8,128)(2,1)}), bf16[1,16,16,576]{3,1,0,2:T(8,128)(2,1)S(1)}, u32[]{:S(2)}, u32[]{:S(2)}) async-start(bf16[1,16,16,576]{3,1,0,2:T(8,128)(2,1)} %reshape.299), calls=%async_computation.2 | async-start | bytes 655360 | tf_op jit(solution)/shard_map/all_to_all | solution.py:120
  152.8 142.9 %all-reduce.3.cloned.1.call-start = ((), (), s32[]{:S(2)}) async-start(), calls=%async_computation.8 | async-start | bytes 5308416
  156.0 7.9 %copy-start.2 = (bf16[1,256,1152]{2,1,0:T(8,128)(2,1)S(1)}, bf16[1,256,1152]{2,1,0:T(8,128)(2,1)}, u32[]{:S(2)}) copy-start(bf16[1,256,1152]{2,1,0:T(8,128)(2,1)} %param.13) | copy-start | bytes 1769476
  166.1 1.0 copy-start.7
  166.1 1.8 copy-start.6
  166.1 237.0 %reduce-scatter.3.cloned.1.call-start = ((), (), s32[]{:S(2)}) async-start(), calls=%async_computation.7 | async-start | bytes 8773632 | tf_op jit(solution)/shard_map/reduce_scatter | solution.py:133
  167.9 1.0 copy-start.8
  174.8 9.0 %collective-permute-start.9 = (bf16[1,1,16,1,1728]{4,0,2,3,1:T(2,128)(2,1)S(1)}, bf16[1,1,16,1,1728]{4,0,2,3,1:T(2,128)(2,1)S(1)}, u32[]{:S(2)}, u32[]{:S(2)}) collective-permute-start(bf16[1,1,16,1,1728]{4,0,2,3,1:T(2,128)(2,1)S(1)} %get-tuple-element.28), channel_id=1, source_target_pairs={{0,10},{1,11},{2,12},{3,13},{4,14},{5,15},{6,0},{7,1},{8,2},{9,3},... | collective-permute-start | bytes 165896 | tf_op jit(solution)/shard_map/ppermute | solution.py:31
  175.2 11.8 %collective-permute-start.8 = (bf16[1,1,16,1,1728]{4,0,2,3,1:T(2,128)(2,1)S(1)}, bf16[1,1,16,1,1728]{4,0,2,3,1:T(2,128)(2,1)S(1)}, u32[]{:S(2)}, u32[]{:S(2)}) collective-permute-start(bf16[1,1,16,1,1728]{4,0,2,3,1:T(2,128)(2,1)S(1)} %get-tuple-element.29), channel_id=1, source_target_pairs={{0,9},{1,10},{2,11},{3,12},{4,13},{5,14},{6,15},{7,0},{8,1},{9,2},... | collective-permute-start | bytes 165896 | tf_op jit(solution)/shard_map/ppermute | solution.py:31
  177.3 33.0 %collective-permute-start.7 = (bf16[1,1,16,1,1728]{4,0,2,3,1:T(2,128)(2,1)S(1)}, bf16[1,1,16,1,1728]{4,0,2,3,1:T(2,128)(2,1)S(1)}, u32[]{:S(2)}, u32[]{:S(2)}) collective-permute-start(bf16[1,1,16,1,1728]{4,0,2,3,1:T(2,128)(2,1)S(1)} %get-tuple-element.30), channel_id=1, source_target_pairs={{0,8},{1,9},{2,10},{3,11},{4,12},{5,13},{6,14},{7,15},{8,0},{9,1},... | collective-permute-start | bytes 165896 | tf_op jit(solution)/shard_map/ppermute | solution.py:31
  177.9 36.0 %collective-permute-start.6 = (bf16[1,1,16,1,1728]{4,0,2,3,1:T(2,128)(2,1)S(1)}, bf16[1,1,16,1,1728]{4,0,2,3,1:T(2,128)(2,1)S(1)}, u32[]{:S(2)}, u32[]{:S(2)}) collective-permute-start(bf16[1,1,16,1,1728]{4,0,2,3,1:T(2,128)(2,1)S(1)} %get-tuple-element.31), channel_id=1, source_target_pairs={{0,7},{1,8},{2,9},{3,10},{4,11},{5,12},{6,13},{7,14},{8,15},{9,0},... | collective-permute-start | bytes 165896 | tf_op jit(solution)/shard_map/ppermute | solution.py:31
  179.5 42.4 %collective-permute-start.5 = (bf16[1,1,16,1,1728]{4,0,2,3,1:T(2,128)(2,1)S(1)}, bf16[1,1,16,1,1728]{4,0,2,3,1:T(2,128)(2,1)S(1)}, u32[]{:S(2)}, u32[]{:S(2)}) collective-permute-start(bf16[1,1,16,1,1728]{4,0,2,3,1:T(2,128)(2,1)S(1)} %get-tuple-element.32), channel_id=1, source_target_pairs={{0,6},{1,7},{2,8},{3,9},{4,10},{5,11},{6,12},{7,13},{8,14},{9,15},... | collective-permute-start | bytes 165896 | tf_op jit(solution)/shard_map/ppermute | solution.py:31
  183.8 41.3 %collective-permute-start.4 = (bf16[1,1,16,1,1728]{4,0,2,3,1:T(2,128)(2,1)S(1)}, bf16[1,1,16,1,1728]{4,0,2,3,1:T(2,128)(2,1)S(1)}, u32[]{:S(2)}, u32[]{:S(2)}) collective-permute-start(bf16[1,1,16,1,1728]{4,0,2,3,1:T(2,128)(2,1)S(1)} %get-tuple-element.33), channel_id=1, source_target_pairs={{0,5},{1,6},{2,7},{3,8},{4,9},{5,10},{6,11},{7,12},{8,13},{9,14},{... | collective-permute-start | bytes 165896 | tf_op jit(solution)/shard_map/ppermute | solution.py:31
  187.0 38.0 %collective-permute-start.3 = (bf16[1,1,16,1,1728]{4,0,2,3,1:T(2,128)(2,1)S(1)}, bf16[1,1,16,1,1728]{4,0,2,3,1:T(2,128)(2,1)S(1)}, u32[]{:S(2)}, u32[]{:S(2)}) collective-permute-start(bf16[1,1,16,1,1728]{4,0,2,3,1:T(2,128)(2,1)S(1)} %get-tuple-element.34), channel_id=1, source_target_pairs={{0,4},{1,5},{2,6},{3,7},{4,8},{5,9},{6,10},{7,11},{8,12},{9,13},{1... | collective-permute-start | bytes 165896 | tf_op jit(solution)/shard_map/ppermute | solution.py:31
  210.3 14.8 %collective-permute-start.2 = (bf16[1,1,16,1,1728]{4,0,2,3,1:T(2,128)(2,1)S(1)}, bf16[1,1,16,1,1728]{4,0,2,3,1:T(2,128)(2,1)S(1)}, u32[]{:S(2)}, u32[]{:S(2)}) collective-permute-start(bf16[1,1,16,1,1728]{4,0,2,3,1:T(2,128)(2,1)S(1)} %get-tuple-element.35), channel_id=1, source_target_pairs={{0,3},{1,4},{2,5},{3,6},{4,7},{5,8},{6,9},{7,10},{8,11},{9,12},{10... | collective-permute-start | bytes 165896 | tf_op jit(solution)/shard_map/ppermute | solution.py:31
  213.9 11.2 %collective-permute-start.1 = (bf16[1,1,16,1,1728]{4,0,2,3,1:T(2,128)(2,1)S(1)}, bf16[1,1,16,1,1728]{4,0,2,3,1:T(2,128)(2,1)S(1)}, u32[]{:S(2)}, u32[]{:S(2)}) collective-permute-start(bf16[1,1,16,1,1728]{4,0,2,3,1:T(2,128)(2,1)S(1)} %get-tuple-element.36), channel_id=1, source_target_pairs={{0,2},{1,3},{2,4},{3,5},{4,6},{5,7},{6,8},{7,9},{8,10},{9,11},{10,... | collective-permute-start | bytes 165896 | tf_op jit(solution)/shard_map/ppermute | solution.py:31
  221.8 8.1 %collective-permute-start = (bf16[1,1,16,1,1728]{4,0,2,3,1:T(2,128)(2,1)S(1)}, bf16[1,1,16,1,1728]{4,0,2,3,1:T(2,128)(2,1)S(1)}, u32[]{:S(2)}, u32[]{:S(2)}) collective-permute-start(bf16[1,1,16,1,1728]{4,0,2,3,1:T(2,128)(2,1)S(1)} %get-tuple-element.37), channel_id=1, source_target_pairs={{0,1},{1,2},{2,3},{3,4},{4,5},{5,6},{6,7},{7,8},{8,9},{9,10},{10,1... | collective-permute-start | bytes 165896 | tf_op jit(solution)/shard_map/ppermute | solution.py:31
  225.0 33.9 %collective-permute-start.12 = (bf16[1,1,16,1,1728]{4,0,2,3,1:T(2,128)(2,1)}, bf16[1,1,16,1,1728]{4,0,2,3,1:T(2,128)(2,1)S(1)}, u32[]{:S(2)}, u32[]{:S(2)}) collective-permute-start(bf16[1,1,16,1,1728]{4,0,2,3,1:T(2,128)(2,1)} %get-tuple-element.25), channel_id=1, source_target_pairs={{0,13},{1,14},{2,15},{3,0},{4,1},{5,2},{6,3},{7,4},{8,5},{9,6},{10... | collective-permute-start | bytes 165896 | tf_op jit(solution)/shard_map/ppermute | solution.py:31
  225.1 29.3 %collective-permute-start.10 = (bf16[1,1,16,1,1728]{4,0,2,3,1:T(2,128)(2,1)}, bf16[1,1,16,1,1728]{4,0,2,3,1:T(2,128)(2,1)S(1)}, u32[]{:S(2)}, u32[]{:S(2)}) collective-permute-start(bf16[1,1,16,1,1728]{4,0,2,3,1:T(2,128)(2,1)} %get-tuple-element.27), channel_id=1, source_target_pairs={{0,11},{1,12},{2,13},{3,14},{4,15},{5,0},{6,1},{7,2},{8,3},{9,4},{... | collective-permute-start | bytes 165896 | tf_op jit(solution)/shard_map/ppermute | solution.py:31
  225.1 31.6 %collective-permute-start.11 = (bf16[1,1,16,1,1728]{4,0,2,3,1:T(2,128)(2,1)}, bf16[1,1,16,1,1728]{4,0,2,3,1:T(2,128)(2,1)S(1)}, u32[]{:S(2)}, u32[]{:S(2)}) collective-permute-start(bf16[1,1,16,1,1728]{4,0,2,3,1:T(2,128)(2,1)} %get-tuple-element.26), channel_id=1, source_target_pairs={{0,12},{1,13},{2,14},{3,15},{4,0},{5,1},{6,2},{7,3},{8,4},{9,5},{1... | collective-permute-start | bytes 165896 | tf_op jit(solution)/shard_map/ppermute | solution.py:31
  225.1 36.1 %collective-permute-start.13 = (bf16[1,1,16,1,1728]{4,0,2,3,1:T(2,128)(2,1)}, bf16[1,1,16,1,1728]{4,0,2,3,1:T(2,128)(2,1)S(1)}, u32[]{:S(2)}, u32[]{:S(2)}) collective-permute-start(bf16[1,1,16,1,1728]{4,0,2,3,1:T(2,128)(2,1)} %get-tuple-element.24), channel_id=1, source_target_pairs={{0,14},{1,15},{2,0},{3,1},{4,2},{5,3},{6,4},{7,5},{8,6},{9,7},{10,... | collective-permute-start | bytes 165896 | tf_op jit(solution)/shard_map/ppermute | solution.py:31
  230.0 0.6 copy-start.12
  230.6 33.0 %collective-permute-start.14 = (bf16[1,1,16,1,1728]{4,0,2,3,1:T(2,128)(2,1)}, bf16[1,1,16,1,1728]{4,0,2,3,1:T(2,128)(2,1)S(1)}, u32[]{:S(2)}, u32[]{:S(2)}) collective-permute-start(bf16[1,1,16,1,1728]{4,0,2,3,1:T(2,128)(2,1)} %get-tuple-element.23), channel_id=1, source_target_pairs={{0,15},{1,0},{2,1},{3,2},{4,3},{5,4},{6,5},{7,6},{8,7},{9,8},{10,9... | collective-permute-start | bytes 165896 | tf_op jit(solution)/shard_map/ppermute | solution.py:31
  270.5 0.7 copy-start.15
  276.0 1.1 copy-start.3
  277.1 1.5 copy-start.1
Sparse Core Ops, SparseCore 0:
  10.1 42.0 all-gather.4
  54.5 53.1 all-gather.2
  166.2 129.4 all-reduce.2
  300.2 102.8 reduce-scatter.2
